TPU v7x, 128 devices: a whole 4x4x4 slice. The times are simulated.
128 devices in a mesh: corpus: 32 (over y, x, core), query: 4 (over z).
Axes of the slice: x: 4, y: 4, z: 4, core: 2. Of those that a mesh axis runs over, the one named last changes fastest.
Arguments:
- corpus_hidden: bfloat16 [1024, 64, 14336], P(('corpus', 'query')), may hold values from -48 to 48
- corpus_grad: bfloat16 [1024, 64, 4096], P(('corpus', 'query')), may hold values from -6 to 6
- corpus_lengths: int32 [1024], P(('corpus', 'query')), may hold values from 16 to 64
- query_hidden: bfloat16 [256, 64, 14336], P(('corpus', 'query')), may hold values from -6 to 6
- query_grad: bfloat16 [256, 64, 4096], P(('corpus', 'query')), may hold values from -6 to 6
- query_lengths: int32 [256], P(('corpus', 'query')), may hold values from 16 to 64
- proj_in: bfloat16 [14336, 64], replicated, may hold values from -0.046875 to 0.046875
- proj_out: bfloat16 [4096, 64], replicated, may hold values from -0.09375 to 0.09375
Outputs:
- scores: float32 [1024, 256], P(('corpus', 'query'))
All inputs are finite; a program needn't handle non-finite values.
Results may differ from a plain program's by a relative error of at most 0.0003.
Values sent between devices are 32-bit elements; how exact they have to be, the bound alone decides.
A program may use at most 128 MiB of HBM per device.

v0:
```python
import jax
import jax.numpy as jnp
from jax import lax
from jax.sharding import PartitionSpec as P


def project(hidden, grad, lengths, proj_in, proj_out):
    slots = lax.broadcasted_iota(jnp.int32, (1, hidden.shape[1]), 1)
    live = (slots < lengths[:, None]).astype(jnp.float32)[:, :, None]
    in_side = jnp.einsum("etf,fk->etk", hidden, proj_in, preferred_element_type=jnp.float32) * live
    out_side = jnp.einsum("etf,fk->etk", grad, proj_out, preferred_element_type=jnp.float32) * live
    grads = jnp.einsum("etk,etj->ekj", out_side, in_side, precision=lax.Precision.HIGHEST)
    return (in_side, out_side, grads)


def invert(fisher):
    width = fisher.shape[0]
    eye = jnp.eye(width, dtype=jnp.float32)
    damped = fisher + 0.1 * jnp.trace(fisher) / width * eye
    factor = jnp.linalg.cholesky(damped)
    return jax.scipy.linalg.cho_solve((factor, True), eye)


def condition(grads, inv_out, inv_in):
    left_done = jnp.einsum("ij,njk->nik", inv_out, grads, precision=lax.Precision.HIGHEST)
    return jnp.einsum("nik,kl->nil", left_done, inv_in, precision=lax.Precision.HIGHEST)


def per_device(
    corpus_hidden,
    corpus_grad,
    corpus_lengths,
    query_hidden,
    query_grad,
    query_lengths,
    proj_in,
    proj_out,
):
    in_corpus, out_corpus, grad_corpus = project(
        corpus_hidden, corpus_grad, corpus_lengths, proj_in, proj_out
    )
    unused_in, unused_out, grad_query = project(
        query_hidden, query_grad, query_lengths, proj_in, proj_out
    )
    part_in = jnp.einsum("etk,etj->kj", in_corpus, in_corpus, precision=lax.Precision.HIGHEST)
    part_out = jnp.einsum("etk,etj->kj", out_corpus, out_corpus, precision=lax.Precision.HIGHEST)
    fisher_in, fisher_out = lax.psum((part_in, part_out), ("corpus", "query"))
    inv_in = invert(fisher_in)
    inv_out = invert(fisher_out)
    corpus_count = grad_corpus.shape[0]
    query_count = grad_query.shape[0]
    left_flat = grad_corpus.reshape(corpus_count, -1)
    right_flat = condition(grad_query, inv_out, inv_in).reshape(query_count, -1)
    group_rows = lax.all_gather(right_flat, "query", axis=0, tiled=True)
    return jnp.einsum(
        "ek,qk->eq",
        left_flat,
        lax.all_gather(group_rows, "corpus", axis=0, tiled=True),
        precision=lax.Precision.HIGHEST,
    )


def solution(mesh):
    placed = (
        P(("corpus", "query"), None, None),
        P(("corpus", "query"), None, None),
        P(("corpus", "query")),
        P(("corpus", "query"), None, None),
        P(("corpus", "query"), None, None),
        P(("corpus", "query")),
        P(),
        P(),
    )
    return jax.shard_map(
        per_device,
        mesh=mesh,
        in_specs=placed,
        out_specs=P(("corpus", "query"), None),
        check_vma=False,
    )
```

profile of v0, /device:TPU:1, one launch (start us, length us, event | category | flops | bytes accessed | tf_op | source)
XLA Modules:
  0.0 187.4 jit_solution(3499629602611967179)
XLA Ops:
  6.5 0.0 copy-start
  6.5 0.0 all-gather.3.cloned.1.call-start
  6.5 0.9 compare_convert_fusion
  7.4 0.7 fusion.24
  8.1 0.0 copy-done
  8.1 0.0 copy-start.1
  8.1 7.4 %fusion.4 = f32[8,64,64]{2,1,0:T(8,128)S(1)} fusion(bf16[8,64,14336]{2,1,0:T(8,128)(2,1)} %param.11, bf16[14336,64]{0,1:T(8,128)(2,1)S(1)} %copy-done, f32[8,64]{1,0:T(8,128)S(1)} %fusion.24), kind=kOutput, calls=%fused_computation.5 | convolution fusion | flops 939556864 | bytes 16648192 | tf_op jit(solution)/shard_map/etf,fk->etk/dot_general | solution.py:10
  15.6 0.0 copy-start.2
  15.6 0.0 copy-start.3
  15.6 0.0 copy-start.4
  15.6 0.6 convolution_bitcast_fusion.3
  16.2 0.0 copy-done.1
  16.2 1.1 fusion.7
  17.3 0.0 copy-done.2
  17.3 0.0 copy-done.3
  17.3 0.4 convolution_multiply_fusion.1
  17.7 0.5 copy-done.4
  18.2 1.2 convolution_multiply_fusion
  19.5 0.6 convolution_bitcast_fusion.4
  20.1 69.2 %all-reduce = (f32[64,64]{0,1:T(8,128)S(1)}, f32[64,64]{0,1:T(8,128)S(1)}) all-reduce(f32[64,64]{0,1:T(8,128)S(1)} %convolution_bitcast_fusion.4, f32[64,64]{0,1:T(8,128)S(1)} %convolution_bitcast_fusion.3), channel_id=1, replica_groups=mesh['corpus'=32,'query'=4] {'corpus','query'}, use_global_device_ids=true, to_apply=%region_0.0 | all-reduce | flops 8192 | bytes 65536 | tf_op jit(solution)/shard_map/psum | solution.py:47
  89.3 0.6 select_reduce_fusion.2
  89.9 0.7 select_reduce_fusion.3
  91.9 0.1 copy.22
  92.0 5.8 %cholesky.55 = f32[64,64]{1,0:T(8,128)S(1)} custom-call(f32[64,64]{1,0:T(8,128)S(1)} %fusion.20), custom_call_target="Cholesky" | custom-call | tf_op jit(solution)/shard_map/jit(cholesky)/cholesky | solution.py:20
  97.9 0.6 compare_reduce_fusion
  98.5 0.7 fusion.17
  99.2 4.9 %custom-call.9 = f32[1,64,64]{1,2,0:T(8,128)S(1)} custom-call(f32[1,64,64]{2,1,0:T(8,128)S(1)} %fusion.17), custom_call_target="InvertDiagBlocksLowerTriangular" | custom-call | tf_op jit(solution)/shard_map/jit(_cho_solve)/triangular_solve | solution.py:21
  104.1 0.3 fusion.12
  104.4 0.2 convolution_bitcast_fusion.1
  104.5 0.1 copy.19
  104.6 5.8 %cholesky.44 = f32[64,64]{1,0:T(8,128)S(1)} custom-call(f32[64,64]{1,0:T(8,128)S(1)} %fusion.23), custom_call_target="Cholesky" | custom-call | tf_op jit(solution)/shard_map/jit(cholesky)/cholesky | solution.py:20
  110.5 0.6 compare_reduce_fusion.1
  111.2 0.7 fusion.16
  111.8 4.9 %custom-call.8 = f32[1,64,64]{1,2,0:T(8,128)S(1)} custom-call(f32[1,64,64]{2,1,0:T(8,128)S(1)} %fusion.16), custom_call_target="InvertDiagBlocksLowerTriangular" | custom-call | tf_op jit(solution)/shard_map/jit(_cho_solve)/triangular_solve | solution.py:21
  116.7 0.3 fusion.14
  117.0 0.2 convolution_bitcast_fusion.2
  117.1 0.3 fusion.26
  117.4 0.2 convolution_bitcast_fusion
  117.6 0.2 fusion.27
  117.8 0.1 reshape.62
  117.9 9.3 %all-gather = f32[4,2,4096]{2,1,0:T(2,128)S(1)} all-gather(f32[1,2,4096]{2,1,0:T(2,128)S(1)} %reshape.62), channel_id=1, replica_groups=mesh['corpus'=32,'query'=4] {'query'}, dimensions={0}, use_global_device_ids=true | all-gather | bytes 163840 | tf_op jit(solution)/shard_map/all_gather | solution.py:54
  127.2 0.7 reshape.63
  128.0 0.0 all-gather.3.cloned.1.call-update
  128.0 0.6 fusion.25
  128.6 0.1 reshape.60
  128.7 45.7 %all-gather.3.cloned.1.call-done = f32[256,4096]{1,0:T(8,128)} async-done(((f32[8,4096]{1,0:T(8,128)}), f32[256,4096]{1,0:T(8,128)}) %all-gather.3.cloned.1.call-update) | async-done | bytes 4194320 | tf_op jit(solution)/shard_map/all_gather | solution.py:58
  174.4 6.1 %fusion.28 = f32[8,256]{1,0:T(8,128)} fusion(f32[8,4096]{1,0:T(8,128)S(1)} %reshape.60, f32[256,4096]{1,0:T(8,128)} %all-gather.3.cloned.1.call-done), kind=kOutput, calls=%fused_computation.48 | convolution fusion | flops 100663296 | bytes 4333568 | tf_op jit(solution)/shard_map/ek,qk->eq/dot_general | solution.py:55
  (5 shorter events, 0.1 us)
Async XLA Ops:
  6.5 1.6 copy-start
  6.5 167.9 %all-gather.3.cloned.1.call-start = ((), (), s32[]{:S(2)}) async-start(), calls=%async_computation | async-start | bytes 4325376 | tf_op jit(solution)/shard_map/all_gather | solution.py:58
  8.1 8.1 %copy-start.1 = (bf16[2,64,14336]{2,1,0:T(8,128)(2,1)S(1)}, bf16[2,64,14336]{2,1,0:T(8,128)(2,1)}, u32[]{:S(2)}) copy-start(bf16[2,64,14336]{2,1,0:T(8,128)(2,1)} %param.14) | copy-start | bytes 11010052
  15.6 1.7 copy-start.2
  15.6 1.7 copy-start.3
  15.6 2.7 %copy-start.4 = (bf16[8,64,4096]{2,1,0:T(8,128)(2,1)S(1)}, bf16[8,64,4096]{2,1,0:T(8,128)(2,1)}, u32[]{:S(2)}) copy-start(bf16[8,64,4096]{2,1,0:T(8,128)(2,1)} %param.12) | copy-start | bytes 12582916
Sparse Core Ops, SparseCore 0:
  128.1 46.2 all-gather.2
where the time goes:
time: 188 us; the launch traced here: 187 us
  blocking collectives  78.5 us (42%)
  waiting for transfers between devices  45.7 us (24%)
  other arithmetic  27 us (14%)
  matrix products  19.6 us (10%)
  between operations  14.9 us (8%)
    psum x1, blocking collectives, per_device(): fisher_in, fisher_out = lax.psum((part_in, part_out), ('corpus', 'query'))  69.2 us
    all_gather x1, waiting for transfers between devices, per_device(): lax.all_gather(group_rows, 'corpus', axis=0, tiled=True)  45.7 us
    another operation x6, other arithmetic, invert(): factor = jnp.linalg.cholesky(damped)  13 us
    another operation x4, other arithmetic, invert(): return jax.scipy.linalg.cho_solve((factor, True), eye)  11.1 us
    all_gather x1, blocking collectives, per_device(): group_rows = lax.all_gather(right_flat, 'query', axis=0, tiled=True)  9.29 us
    dot_general x2, matrix products, project(): jnp.einsum('etf,fk->etk', hidden, proj_in, preferred_element_type=jnp.flo...  8.52 us
    dot_general x1, matrix products, per_device(): jnp.einsum('ek,qk->eq', left_flat, lax.all_gather(group_rows, 'corpus', a...  6.14 us
  transfers between devices with their start and end apart: 1, of which 1 were waited for; matrix products, arithmetic and copies ran while one was open for 0% of the time, Pallas kernels for 0%

commit v1 on v0

v1 whole, which is shorter than its diff:
```python
import jax
import jax.numpy as jnp
from jax import lax
from jax.experimental import pallas as pl
from jax.experimental.pallas import tpu as pltpu
from jax.sharding import PartitionSpec as P

F32 = jnp.float32
BF16 = jnp.bfloat16
HIGHEST = lax.Precision.HIGHEST
MESH = pl.DeviceIdType.MESH
BY_ROWS = (((1,), (1,)), ((), ()))
BY_TOKENS = (((0,), (0,)), ((), ()))

RANK = 64
LEN = 64
SIDE = 4
CHIPS = SIDE * SIDE
MEMBERS = 2 * SIDE
DEVICES = CHIPS * MEMBERS

PARTS = ((0, 24, (2, 1, 0)), (24, 24, (1, 0, 2)), (48, 16, (0, 2, 1)))


def coordinates():
    corpus = lax.axis_index("corpus")
    z = lax.axis_index("query")
    return corpus % 2, (corpus // 2) % SIDE, corpus // (2 * SIDE), z


def device(core, y, x, z):
    return ((y * SIDE + x) * 2 + core, z)


def iota(shape, axis):
    return lax.broadcasted_iota(jnp.int32, shape, axis)


def spread(block, row):
    return jnp.broadcast_to(block[row : row + 1], block.shape)


def exact_dot(a, b, dims):
    return lax.dot_general(a, b, dims, precision=HIGHEST, preferred_element_type=F32)


def plain_dot(a, b, dims):
    return lax.dot_general(a, b, dims, preferred_element_type=F32)


def damp(fisher):
    row, lane = iota(fisher.shape, 0), iota(fisher.shape, 1)
    diag_in = row == lane
    diag_out = row + RANK == lane
    trace_in = jnp.sum(jnp.where(diag_in, fisher, 0.0))
    trace_out = jnp.sum(jnp.where(diag_out, fisher, 0.0))
    fisher = fisher + jnp.where(diag_in, 0.1 * trace_in / RANK, 0.0)
    return fisher + jnp.where(diag_out, 0.1 * trace_out / RANK, 0.0)


def invert_pair(pair):
    step = 8
    count = RANK // step
    shape = (step, 2 * RANK)
    rows = [pair[step * i : step * (i + 1)] for i in range(count)]
    lane, row = iota(shape, 1), iota(shape, 0)
    column = lane % RANK
    for b in range(count):
        inside = (column >= step * b) & (column < step * (b + 1))
        picked = [
            [
                jnp.take_along_axis(rows[o], jnp.where(lane < RANK, step * b + j, RANK + step * b + j), axis=1)
                for j in range(step)
            ]
            for o in range(count)
        ]
        d = [[spread(picked[b][j], i) if j >= i else None for j in range(step)] for i in range(step)]
        r = [
            jnp.where(inside, jnp.where(column == step * b + i, 1.0, 0.0), spread(rows[b], i))
            for i in range(step)
        ]
        for k in range(step):
            pivot = 1.0 / d[k][k]
            u = [None] * step
            for j in range(k + 1, step):
                u[j] = d[k][j] * pivot
            for i in range(k + 1, step):
                for j in range(i, step):
                    d[i][j] = d[i][j] - u[i] * d[k][j]
                r[i] = r[i] - u[i] * r[k]
            r[k] = r[k] * pivot
            for j in range(k + 1, step):
                d[k][j] = u[j]
        for k in range(step - 1, 0, -1):
            for i in range(k):
                r[i] = r[i] - d[i][k] * r[k]
        for o in range(count):
            if o == b:
                block = r[0]
                for i in range(1, step):
                    block = jnp.where(row == i, r[i], block)
                rows[o] = block
                continue
            t = [picked[o][j] * r[j] for j in range(step)]
            total = ((t[0] + t[1]) + (t[2] + t[3])) + ((t[4] + t[5]) + (t[6] + t[7]))
            rows[o] = jnp.where(inside, 0.0, rows[o]) - total
    return jnp.concatenate(rows, axis=0)


def split(values):
    high = values.astype(BF16)
    low = (values - high.astype(F32)).astype(BF16)
    return high, low


OUT_CUTS = ((0, 2048), (2048, 2048))
IN_CUTS = ((0, 4096), (4096, 4096), (8192, 4096), (12288, 2048))


def kernel(
    corpus_hidden,
    corpus_grad,
    corpus_lengths,
    query_hidden,
    query_grad,
    query_lengths,
    proj_in,
    proj_out,
    out,
    v_ch,
    v_cg,
    v_qh,
    v_qg,
    v_pin,
    v_pout,
    grads,
    slabs,
    q_high,
    q_low,
    part,
    piece,
    from_members,
    from_plane,
    fisher,
    turned,
    local_sem,
    sum_send,
    sum_recv,
    slab_send,
    slab_recv,
    pair_send,
    pair_recv,
):
    core, x, y, z = coordinates()
    me = (y, x, z)
    member, place = core * SIDE + z, y * SIDE + x
    examples = corpus_hidden.shape[0] // LEN
    queries = query_hidden.shape[0] // LEN

    copies = {}

    def bring(name, src, dst, cut):
        at, width = cut
        copy = pltpu.make_async_copy(
            src.at[:, pl.ds(at, width)], dst.at[:, pl.ds(at, width)], local_sem.at[len(copies)]
        )
        copy.start()
        copies[name, at] = copy

    for cut in OUT_CUTS:
        bring("pout", proj_out, v_pout, cut)
        bring("qg", query_grad, v_qg, cut)
    for cut in IN_CUTS:
        bring("pin", proj_in, v_pin, cut)
        bring("qh", query_hidden, v_qh, cut)
    for cut in OUT_CUTS:
        bring("cg", corpus_grad, v_cg, cut)
    for cut in IN_CUTS:
        bring("ch", corpus_hidden, v_ch, cut)

    barrier = pltpu.get_barrier_semaphore()

    def member_at(d):
        t = (member + d) % MEMBERS
        return device(t // SIDE, y, x, t % SIDE)

    def place_at(d):
        t = (place + d) % CHIPS
        return device(core, t // SIDE, t % SIDE, z)

    for d in range(1, MEMBERS):
        pl.semaphore_signal(barrier, inc=1, device_id=member_at(d), device_id_type=MESH)
    for d in range(1, CHIPS):
        pl.semaphore_signal(barrier, inc=1, device_id=place_at(d), device_id_type=MESH)

    def projected(name, src, weight_name, weight, cuts):
        total = None
        for at, width in cuts:
            if weight_name:
                copies[weight_name, at].wait()
            copies[name, at].wait()
            term = plain_dot(src[:, pl.ds(at, width)], weight[:, pl.ds(at, width)], BY_ROWS)
            total = term if total is None else total + term
        return total

    slot = iota((LEN, RANK), 0)

    def masked(values, lengths, count):
        return [
            jnp.where(slot < lengths[e], values[e * LEN : (e + 1) * LEN], 0.0) for e in range(count)
        ]

    out_query = masked(projected("qg", v_qg, "pout", v_pout, OUT_CUTS), query_lengths, queries)
    in_query = masked(projected("qh", v_qh, "pin", v_pin, IN_CUTS), query_lengths, queries)
    lower = iota((RANK // 2, 2 * RANK), 1) < RANK
    mine = slabs.at[y, x, core, z]
    for q in range(queries):
        turned[pl.ds(0, RANK), :] = exact_dot(
            out_query[q], jnp.concatenate([in_query[q], in_query[q]], axis=1), BY_TOKENS
        )
        even = turned[pl.ds(0, RANK // 2, stride=2), :]
        odd = turned[pl.ds(1, RANK // 2, stride=2), :]
        mine[pl.ds(q * RANK // 2, RANK // 2), :] = jnp.where(lower, even, odd)

    pl.semaphore_wait(barrier, MEMBERS - 1 + CHIPS - 1)

    def neighbour(axis, d):
        there = list(me)
        there[axis] = (there[axis] + d) % SIDE
        return device(core, *there)

    def block(p, phase, at, whose):
        first, count, order = PARTS[p]
        index = [pl.ds(0, SIDE) if k in order[:phase] else me[k] for k in range(3)]
        index[order[phase]] = at
        return slabs.at[index[0], index[1], whose, index[2], pl.ds(first, count)]

    def send_block(p, phase):
        axis = PARTS[p][2][phase]
        ref = block(p, phase, me[axis], core)
        for d in (2, 1, 3):
            pltpu.make_async_remote_copy(
                src_ref=ref,
                dst_ref=ref,
                send_sem=slab_send.at[p, phase],
                recv_sem=slab_recv.at[p, phase],
                device_id=neighbour(axis, d),
                device_id_type=MESH,
            ).start()

    def wait_block(p, phase, sem):
        ref = block(p, phase, pl.ds(0, SIDE - 1), core)
        pltpu.make_async_copy(ref, ref, sem.at[p, phase]).wait()

    def pair_copy(p):
        first, count, _ = PARTS[p]
        ref = slabs.at[:, :, core, :, pl.ds(first, count)]
        return pltpu.make_async_remote_copy(
            src_ref=ref,
            dst_ref=ref,
            send_sem=pair_send.at[p],
            recv_sem=pair_recv.at[p],
            device_id=device(1 - core, y, x, z),
            device_id_type=MESH,
        )

    everyone = range(len(PARTS))
    for p in everyone:
        send_block(p, 0)

    outs = masked(projected("cg", v_cg, None, v_pout, OUT_CUTS), corpus_lengths, examples)
    ins = projected("ch", v_ch, None, v_pin, IN_CUTS[:2])
    for p in everyone:
        wait_block(p, 0, slab_recv)
        send_block(p, 1)
    ins = ins + projected("ch", v_ch, None, v_pin, IN_CUTS[2:])
    ins = masked(ins, corpus_lengths, examples)
    both = jnp.concatenate(
        [jnp.concatenate([i, o], axis=1) for i, o in zip(ins, outs)], axis=0
    )
    gram = exact_dot(both, both, BY_TOKENS)
    lower = iota((RANK, 2 * RANK), 1) < RANK
    part[...] = jnp.where(lower, gram[:RANK], gram[RANK:])

    def octet(t):
        return pl.ds(pl.multiple_of(t * 8, 8), 8)

    def send_sum(stage, src, dst, to):
        pltpu.make_async_remote_copy(
            src_ref=src,
            dst_ref=dst,
            send_sem=sum_send.at[stage],
            recv_sem=sum_recv.at[stage],
            device_id=to,
            device_id_type=MESH,
        ).start()

    def wait_all(ref, sem):
        pltpu.make_async_copy(ref, ref, sem).wait()

    for d in range(1, MEMBERS):
        send_sum(0, part.at[octet((member + d) % MEMBERS)], from_members.at[d - 1], member_at(d))
    for e in range(examples):
        grads[pl.ds(e * RANK, RANK), :] = exact_dot(outs[e], ins[e], BY_TOKENS)
    for p in everyone:
        wait_block(p, 1, slab_recv)
        send_block(p, 2)
    wait_all(from_members, sum_recv.at[0])
    total = part[octet(member), :]
    for d in range(MEMBERS - 1):
        total = total + from_members[d]
    piece[...] = total
    for d in range(1, CHIPS):
        send_sum(1, piece, from_plane.at[d - 1], place_at(d))
    wait_all(from_plane, sum_recv.at[1])
    for d in range(CHIPS - 1):
        total = total + from_plane[d]
    fisher[octet(member), :] = total
    for d in range(1, MEMBERS):
        send_sum(2, fisher.at[octet(member)], fisher.at[octet(member)], member_at(d))
    for p in everyone:
        wait_block(p, 2, slab_recv)
        pair_copy(p).start()
    wait_all(from_members, sum_recv.at[2])

    inverse = invert_pair(damp(fisher[...]))
    swapped = pltpu.roll(inverse, RANK, 1)
    twice_in = jnp.where(lower, inverse, swapped)
    right_done = exact_dot(grads[...], twice_in, (((1,), (0,)), ((), ())))
    right_done = jnp.concatenate(
        [right_done[e * RANK : (e + 1) * RANK] for e in range(examples)], axis=1
    )
    done = exact_dot(swapped[:, :RANK], right_done, (((1,), (0,)), ((), ())))
    for e in range(examples):
        turned[pl.ds(e * RANK, RANK), :] = done[:, e * 2 * RANK : (e + 1) * 2 * RANK]
    lower = iota((examples, 2 * RANK), 1) < RANK
    left = jnp.concatenate(
        [
            jnp.where(
                lower,
                turned[pl.ds(i, examples, stride=RANK), :],
                turned[pl.ds(i + 1, examples, stride=RANK), :],
            )
            for i in range(0, RANK, 2)
        ],
        axis=1,
    )
    left_high = left.astype(BF16).astype(F32)
    left_both = jnp.concatenate([left_high, left - left_high], axis=0).astype(BF16)

    for p in everyone:
        pair_copy(p).wait_recv()
    flat = slabs.reshape(DEVICES * RANK, 2 * RANK)
    half = RANK // 2
    for q in range(queries):
        for i in range(half):
            high, low = split(flat[pl.ds(q * half + i, DEVICES, stride=RANK), :])
            q_high[pl.ds(q * DEVICES, DEVICES), pl.ds(i * 2 * RANK, 2 * RANK)] = high
            q_low[pl.ds(q * DEVICES, DEVICES), pl.ds(i * 2 * RANK, 2 * RANK)] = low
    main = plain_dot(q_high[...], left_both, BY_ROWS)
    rest = plain_dot(q_low[...], left_both, BY_ROWS)
    main = main.T
    rest = rest.T
    scores = main[:examples] + main[examples:] + rest[:examples]
    out[...] = scores

    for p in everyone:
        for phase in range(3):
            wait_block(p, phase, slab_send)
        pair_copy(p).wait_send()
    wait_all(from_members, sum_send.at[0])
    wait_all(from_plane, sum_send.at[1])
    wait_all(from_members, sum_send.at[2])


def per_device(
    corpus_hidden,
    corpus_grad,
    corpus_lengths,
    query_hidden,
    query_grad,
    query_lengths,
    proj_in,
    proj_out,
):
    examples = corpus_hidden.shape[0]
    queries = query_hidden.shape[0]
    flat = lambda a: a.reshape(-1, a.shape[-1])
    anywhere = pl.BlockSpec(memory_space=pl.ANY)
    scalars = pl.BlockSpec(memory_space=pltpu.SMEM)
    operands = (
        flat(corpus_hidden),
        flat(corpus_grad),
        corpus_lengths,
        flat(query_hidden),
        flat(query_grad),
        query_lengths,
        proj_in.T,
        proj_out.T,
    )
    big = [operands[k] for k in (0, 1, 3, 4, 6, 7)]
    dma = pltpu.SemaphoreType.DMA
    scores = pl.pallas_call(
        kernel,
        out_shape=jax.ShapeDtypeStruct((examples, queries * DEVICES), F32),
        in_specs=[anywhere, anywhere, scalars, anywhere, anywhere, scalars, anywhere, anywhere],
        out_specs=pl.BlockSpec(memory_space=pltpu.VMEM),
        scratch_shapes=[pltpu.VMEM(a.shape, BF16) for a in big]
        + [
            pltpu.VMEM((examples * RANK, RANK), F32),
            pltpu.VMEM((SIDE, SIDE, 2, SIDE, RANK, 2 * RANK), F32),
            pltpu.VMEM((queries * DEVICES, RANK * RANK), BF16),
            pltpu.VMEM((queries * DEVICES, RANK * RANK), BF16),
            pltpu.VMEM((RANK, 2 * RANK), F32),
            pltpu.VMEM((8, 2 * RANK), F32),
            pltpu.VMEM((MEMBERS - 1, 8, 2 * RANK), F32),
            pltpu.VMEM((CHIPS - 1, 8, 2 * RANK), F32),
            pltpu.VMEM((RANK, 2 * RANK), F32),
            pltpu.VMEM((examples * RANK, 2 * RANK), F32),
            dma((24,)),
            dma((3,)),
            dma((3,)),
            dma((3, 3)),
            dma((3, 3)),
            dma((3,)),
            dma((3,)),
        ],
        compiler_params=pltpu.CompilerParams(
            collective_id=0, has_side_effects=True, vmem_limit_bytes=60 * 1024 * 1024
        ),
        name="influence",
    )(*operands)
    return scores.reshape(examples, queries, DEVICES).transpose(0, 2, 1).reshape(examples, -1)


def solution(mesh):
    placed = (
        P(("corpus", "query"), None, None),
        P(("corpus", "query"), None, None),
        P(("corpus", "query")),
        P(("corpus", "query"), None, None),
        P(("corpus", "query"), None, None),
        P(("corpus", "query")),
        P(),
        P(),
    )
    return jax.shard_map(
        per_device,
        mesh=mesh,
        in_specs=placed,
        out_specs=P(("corpus", "query"), None),
        check_vma=False,
    )
```

time: 188 us -> 47.1 us (0.25)
  blocking collectives: 78.5 us -> 0 us
  waiting for transfers between devices: 45.7 us -> 0 us
  Pallas kernels: 0 us -> 45.4 us
  other arithmetic: 27 us -> 0 us
  matrix products: 19.6 us -> 0 us
  between operations: 14.9 us -> 0.02 us
    psum x1 -> x0, blocking collectives: 69.2 us -> none  [per_device(): fisher_in, fisher_out = lax.psum((part_in, part_out), ('corpus', 'query'))]
    all_gather x1 -> x0, waiting for transfers between devices: 45.7 us -> none  [per_device(): lax.all_gather(group_rows, 'corpus', axis=0, tiled=True)]
    pallas_call x0 -> x1, Pallas kernels: none -> 45.4 us  [per_device(): pl.pallas_call(kernel, out_shape=jax.ShapeDtypeStruct((examples, queries...]
    another operation x10 -> x0, other arithmetic: 24.1 us -> none  [the longest x6 13 us: invert(): factor = jnp.linalg.cholesky(damped)]
    dot_general x11 -> x0, matrix products: 18.7 us -> none  [the longest x2 8.52 us: project(): jnp.einsum('etf,fk->etk', hidden, proj_in, preferred_element_type=jnp.flo...]
    all_gather x1 -> x0, blocking collectives: 9.29 us -> none  [per_device(): group_rows = lax.all_gather(right_flat, 'query', axis=0, tiled=True)]
  transfers between devices with their start and end apart: 1 -> 0, of which waited for: 1 -> 0; matrix products, arithmetic and copies ran while one was open for 0% -> 0% of each run, Pallas kernels for 0% -> 0%
where the time goes in v1:
time: 47.1 us; the launch traced here: 47 us
  Pallas kernels  45.4 us (96%)
  local copies, waits for them, and re-layouts  1.51 us (3%)
    pallas_call x1, Pallas kernels, per_device(): pl.pallas_call(kernel, out_shape=jax.ShapeDtypeStruct((examples, queries...  45.4 us
    reshape x2, local copies, waits for them, and re-layouts, per_device(): scores.reshape(examples, queries, DEVICES).transpose(0, 2, 1)  1.51 us

profile of v1, /device:TPU:1, one launch (start us, length us, event | category | flops | bytes accessed | tf_op | source)
XLA Modules:
  0.0 47.0 jit_solution(1506925011318201405)
XLA Ops:
  0.0 45.4 %influence.1 = f32[8,256]{1,0:T(8,128)} custom-call(bf16[512,14336]{1,0:T(8,128)(2,1)} %bitcast.10, bf16[512,4096]{1,0:T(8,128)(2,1)} %bitcast.11, s32[8]{0:T(128)} %corpus_lengths.1, bf16[128,14336]{1,0:T(8,128)(2,1)} %bitcast.12, bf16[128,4096]{1,0:T(8,128)(2,1)} %bitcast.14, s32[2]{0:T(128)} %query_lengths.1, bf16[64,14336]{1,0:T(8,128)(2,1)} %bitcast.13, ...), custom_call_target="tpu_custom_call" | custom-call | tf_op jit(solution)/shard_map/influence/pallas_call | solution.py:403
  45.4 0.8 %copy.10 = f32[8,2,128]{0,1,2:T(2,128)S(1)} copy(f32[8,2,128]{2,0,1:T(8,128)} %bitcast.17) | data formatting | bytes 16384 | tf_op jit(solution)/shard_map/reshape | solution.py:433
  46.3 0.7 %copy.11 = f32[8,256]{1,0:T(8,128)} copy(f32[8,256]{0,1:T(8,128)S(1)} %bitcast.16) | data formatting | bytes 16384 | tf_op jit(solution)/shard_map/reshape | solution.py:433

commit v2 on v1

v2 whole, which is shorter than its diff:
```python
import jax
import jax.numpy as jnp
from jax import lax
from jax.experimental import pallas as pl
from jax.experimental.pallas import tpu as pltpu
from jax.sharding import PartitionSpec as P

F32 = jnp.float32
BF16 = jnp.bfloat16
MESH = pl.DeviceIdType.MESH
BY_ROWS = (((1,), (1,)), ((), ()))
BY_COLUMNS = (((1,), (0,)), ((), ()))

RANK = 64
LEN = 64
SIDE = 4
CHIPS = SIDE * SIDE
MEMBERS = 2 * SIDE
DEVICES = CHIPS * MEMBERS

PARTS = ((0, 24, (2, 1, 0)), (24, 24, (1, 0, 2)), (48, 16, (0, 2, 1)))
EVERYONE = range(len(PARTS))
STEPS = (1, 3, 2)


def coordinates():
    corpus = lax.axis_index("corpus")
    z = lax.axis_index("query")
    return corpus % 2, (corpus // 2) % SIDE, corpus // (2 * SIDE), z


def device(core, y, x, z):
    return ((y * SIDE + x) * 2 + core, z)


def iota(shape, axis):
    return lax.broadcasted_iota(jnp.int32, shape, axis)


def spread(block, row):
    return jnp.broadcast_to(block[row : row + 1], block.shape)


def plain_dot(a, b, dims):
    return lax.dot_general(a, b, dims, preferred_element_type=F32)


def damp(fisher):
    row, lane = iota(fisher.shape, 0), iota(fisher.shape, 1)
    diag = row == lane % RANK
    held = jnp.sum(jnp.where(diag, fisher, 0.0), axis=0, keepdims=True)
    lower = iota(held.shape, 1) < RANK
    trace_in = jnp.sum(jnp.where(lower, held, 0.0), axis=1, keepdims=True)
    trace_out = jnp.sum(jnp.where(lower, 0.0, held), axis=1, keepdims=True)
    shift = 0.1 / RANK * jnp.where(lower, trace_in, trace_out)
    return fisher + jnp.where(diag, shift, 0.0)


def invert_pair(pair):
    step = 8
    count = RANK // step
    shape = (step, 2 * RANK)
    lane, row = iota(shape, 1), iota(shape, 0)
    column = lane % RANK

    def eliminate(b, carry):
        first = pl.multiple_of(b * step, step)
        panel_at = pl.ds(first, step)
        offset = column - first
        inside = (offset >= 0) & (offset < step)
        where_j = [jnp.where(lane < RANK, 0, RANK) + first + j for j in range(step)]
        pick = lambda block: [jnp.take_along_axis(block, at, axis=1) for at in where_j]
        panel = pair[panel_at, :]
        picked = pick(panel)
        d = [[spread(picked[j], i) if j >= i else None for j in range(step)] for i in range(step)]
        r = [jnp.where(inside, jnp.where(offset == i, 1.0, 0.0), spread(panel, i)) for i in range(step)]
        for k in range(step):
            pivot = 1.0 / d[k][k]
            u = [None] * step
            for j in range(k + 1, step):
                u[j] = d[k][j] * pivot
            for i in range(k + 1, step):
                for j in range(i, step):
                    d[i][j] = d[i][j] - u[i] * d[k][j]
                r[i] = r[i] - u[i] * r[k]
            r[k] = r[k] * pivot
            for j in range(k + 1, step):
                d[k][j] = u[j]
        for k in range(step - 1, 0, -1):
            for i in range(k):
                r[i] = r[i] - d[i][k] * r[k]
        for o in range(count):
            at = pl.ds(o * step, step)
            block = pair[at, :]
            t = [c * rj for c, rj in zip(pick(block), r)]
            total = ((t[0] + t[1]) + (t[2] + t[3])) + ((t[4] + t[5]) + (t[6] + t[7]))
            pair[at, :] = jnp.where(inside, 0.0, block) - total
        block = r[0]
        for i in range(1, step):
            block = jnp.where(row == i, r[i], block)
        pair[panel_at, :] = block
        return carry

    lax.fori_loop(0, count, eliminate, 0)


def split(values):
    high = values.astype(BF16)
    low = (values - high.astype(F32)).astype(BF16)
    return high, low


def left_of(values, axis):
    high, low = split(values)
    return jnp.concatenate([high, low, high], axis=axis)


def right_of(values, axis):
    high, low = split(values)
    return jnp.concatenate([high, high, low], axis=axis)


def gradients(out_side, in_side):
    lower = iota(out_side.shape, 1) < LEN
    left = jnp.concatenate(
        [left_of(jnp.where(lower, out_side, 0.0), 1), left_of(jnp.where(lower, 0.0, out_side), 1)], axis=0
    )
    right = right_of(in_side, 1)
    return plain_dot(left, jnp.concatenate([right, right], axis=0), BY_ROWS)


OUT_CUTS = ((0, 4096, 1),)
QUERY_CUTS = ((0, 3584, 4),)
CORPUS_CUTS = ((0, 4096, 1), (4096, 4096, 2), (12288, 2048, 1))


def kernel(
    corpus_hidden,
    corpus_grad,
    corpus_lengths,
    query_hidden,
    query_grad,
    query_lengths,
    proj_in,
    proj_out,
    out,
    v_ch,
    v_cg,
    v_qh,
    v_qg,
    v_pin,
    v_pout,
    in_corpus,
    out_corpus,
    in_query,
    out_query,
    grads,
    slabs,
    q_high,
    q_low,
    part,
    piece,
    from_members,
    from_plane,
    fisher,
    turned,
    ahead,
    query_sem,
    corpus_sem,
    weight_sem,
    sum_send,
    sum_recv,
    slab_send,
    slab_recv,
    pair_send,
    pair_recv,
):
    core, x, y, z = coordinates()
    me = (y, x, z)
    member, place = core * SIDE + z, y * SIDE + x
    examples = corpus_hidden.shape[0] // LEN
    queries = query_hidden.shape[0] // LEN

    def bring(one, cut, k):
        src, dst, sem, first = one
        begin, width, _ = cut
        at = pl.ds(pl.multiple_of(begin + k * width, width), width)
        return pltpu.make_async_copy(src.at[:, at], dst.at[:, at], sem.at[first + begin // 1024 + k])

    def bring_all(cuts, *what):
        for cut in cuts:

            def start(k, carry):
                for one in what:
                    bring(one, cut, k).start()
                return carry

            lax.fori_loop(0, cut[2], start, 0)

    last = proj_in.shape[1] // 1024
    pout = (proj_out, v_pout, weight_sem, last)
    pin = (proj_in, v_pin, weight_sem, 0)
    qg = (query_grad, v_qg, query_sem, last)
    qh = (query_hidden, v_qh, query_sem, 0)
    cg = (corpus_grad, v_cg, corpus_sem, last)
    ch = (corpus_hidden, v_ch, corpus_sem, 0)
    bring_all(OUT_CUTS, pout, qg)
    bring_all(QUERY_CUTS, pin, qh)
    bring_all(OUT_CUTS, cg)
    bring_all(CORPUS_CUTS, ch)

    barrier = pltpu.get_barrier_semaphore()

    def member_at(d):
        t = (member + d) % MEMBERS
        return device(t // SIDE, y, x, t % SIDE)

    def place_at(d):
        t = (place + d) % CHIPS
        return device(core, t // SIDE, t % SIDE, z)

    for d in range(1, MEMBERS):
        pl.semaphore_signal(barrier, inc=1, device_id=member_at(d), device_id_type=MESH)
    for d in range(1, CHIPS):
        pl.semaphore_signal(barrier, inc=1, device_id=place_at(d), device_id_type=MESH)

    def project(what, weight, total, cuts, also=None):
        for cut in cuts:
            begin, width, count = cut

            def step(k, carry):
                for one in (what, also) if also else (what,):
                    bring(one, cut, k).wait()
                at = pl.ds(pl.multiple_of(begin + k * width, width), width)
                total[...] += plain_dot(what[1][:, at], weight[:, at], BY_ROWS)
                return carry

            lax.fori_loop(0, count, step, 0)

    def clear(total):
        total[...] = jnp.zeros_like(total)

    def sides(in_total, out_total, lengths, count):
        slot = iota((LEN, 2 * RANK), 0)
        both = jnp.concatenate([in_total[...], out_total[...]], axis=1)
        both = [
            jnp.where(slot < lengths[e], both[e * LEN : (e + 1) * LEN], 0.0) for e in range(count)
        ]
        return jnp.concatenate(both, axis=0).T

    for total in (out_query, in_query, out_corpus, in_corpus):
        clear(total)
    project(qg, v_pout, out_query, OUT_CUTS, pout)
    project(qh, v_pin, in_query, QUERY_CUTS, pin)
    both = sides(in_query, out_query, query_lengths, queries)
    half = RANK // 2
    lower = iota((half, 2 * RANK), 1) < RANK
    mine = slabs.at[core, y, x, z]
    turned[pl.ds(0, queries * RANK), :] = gradients(both[RANK:], both[:RANK])
    for q in range(queries):
        even = turned[pl.ds(q * RANK, half, stride=2), :]
        odd = turned[pl.ds(q * RANK + 1, half, stride=2), :]
        mine[pl.ds(q * half, half), :] = jnp.where(lower, even, odd)

    pl.semaphore_wait(barrier, MEMBERS - 1 + CHIPS - 1)

    def block(p, places, whose=core):
        first, count, order = PARTS[p]
        index = [None] * 3
        for axis, place in zip(order, places):
            index[axis] = place
        return slabs.at[whose, index[0], index[1], index[2], pl.ds(first, count)]

    def own(p, phase, d=0):
        return (me[PARTS[p][2][phase]] + SIDE - d) % SIDE

    def to_axis(p, phase, ref, d, sem):
        there = list(me)
        axis = PARTS[p][2][phase]
        there[axis] = (there[axis] + d) % SIDE
        pltpu.make_async_remote_copy(
            src_ref=ref,
            dst_ref=ref,
            send_sem=slab_send.at[p, sem],
            recv_sem=slab_recv.at[p, sem],
            device_id=device(core, *there),
            device_id_type=MESH,
        ).start()

    def to_sibling(p, ref):
        pltpu.make_async_remote_copy(
            src_ref=ref,
            dst_ref=ref,
            send_sem=pair_send.at[p],
            recv_sem=pair_recv.at[p],
            device_id=device(1 - core, y, x, z),
            device_id_type=MESH,
        ).start()

    def wait_all(ref, sem):
        pltpu.make_async_copy(ref, ref, sem).wait()

    every = pl.ds(0, SIDE)
    others = pl.ds(0, SIDE - 1)

    def first_phase():
        for p in EVERYONE:
            ref = block(p, (own(p, 0), own(p, 1), own(p, 2)))
            for d in STEPS:
                to_axis(p, 0, ref, d, 0)

    def second_phase():
        for p in EVERYONE:
            wait_all(block(p, (others, 0, 0)), slab_recv.at[p, 0])
            ref = block(p, (every, own(p, 1), own(p, 2)))
            for d in STEPS:
                to_axis(p, 1, ref, d, d)
            for d in STEPS:
                to_axis(p, 2, ref, d, 3 + d)
            to_sibling(p, ref)

    def third_phase(d):
        for p in EVERYONE:
            ref = block(p, (every, own(p, 1, d), own(p, 2)))
            wait_all(ref, slab_recv.at[p, d])
            for far in STEPS:
                to_axis(p, 2, ref, far, 3 + far)
            to_sibling(p, ref)

    def last_phase(d):
        for p in EVERYONE:
            ref = block(p, (every, every, own(p, 2, d)))
            wait_all(ref, slab_recv.at[p, 3 + d])
            to_sibling(p, ref)

    first_phase()

    project(cg, v_pout, out_corpus, OUT_CUTS)
    project(ch, v_pin, in_corpus, CORPUS_CUTS[:1])
    second_phase()
    project(ch, v_pin, in_corpus, CORPUS_CUTS[1:])
    both = sides(in_corpus, out_corpus, corpus_lengths, examples)
    gram = plain_dot(left_of(both, 1), right_of(both, 1), BY_ROWS)
    lower = iota((RANK, 2 * RANK), 1) < RANK
    part[...] = jnp.where(lower, gram[:RANK], gram[RANK:])

    def octet(t):
        return pl.ds(pl.multiple_of(t * 8, 8), 8)

    def send_sum(stage, src, dst, to):
        pltpu.make_async_remote_copy(
            src_ref=src,
            dst_ref=dst,
            send_sem=sum_send.at[stage],
            recv_sem=sum_recv.at[stage],
            device_id=to,
            device_id_type=MESH,
        ).start()

    for d in range(1, MEMBERS):
        send_sum(0, part.at[octet((member + d) % MEMBERS)], from_members.at[d - 1], member_at(d))
    for d in STEPS:
        third_phase(d)
    for e in range(0, examples, 2):
        tokens = slice(e * LEN, (e + 2) * LEN)
        grads[pl.ds(e * RANK, 2 * RANK), :] = gradients(both[RANK:, tokens], both[:RANK, tokens])
    wait_all(from_members, sum_recv.at[0])
    total = part[octet(member), :]
    for d in range(MEMBERS - 1):
        total = total + from_members[d]
    piece[...] = total
    for d in range(1, CHIPS):
        send_sum(1, piece, from_plane.at[d - 1], place_at(d))
    last_phase(1)
    wait_all(from_plane, sum_recv.at[1])
    for d in range(CHIPS - 1):
        total = total + from_plane[d]
    fisher[octet(member), :] = total
    for d in range(1, MEMBERS):
        send_sum(2, fisher.at[octet(member)], fisher.at[octet(member)], member_at(d))

    for d in STEPS[1:]:
        last_phase(d)
    flat = slabs.reshape(DEVICES * RANK, 2 * RANK)

    def halve(row):
        q, i = row // half, row % half
        high, low = split(flat[pl.ds(row, DEVICES, stride=RANK), :].T)
        at = (
            pl.ds(pl.multiple_of(i * 2 * RANK, 2 * RANK), 2 * RANK),
            pl.ds(pl.multiple_of(q * DEVICES, DEVICES), DEVICES),
        )
        q_high[at] = high
        q_low[at] = low

    def halve_some(b):
        for k in range(8):
            halve(b * 8 + k)

    for p in EVERYONE:
        wait_all(block(p, (every, every, every), 0), pair_recv.at[p])
    lax.fori_loop(0, RANK // 8, lambda b, carry: (halve_some(b), carry)[1], 0)

    wait_all(from_members, sum_recv.at[2])
    pair = turned.at[pl.ds(0, RANK)]
    pair[...] = damp(fisher[...])
    invert_pair(pair)
    inverse = pair[...]
    swapped = pltpu.roll(inverse, RANK, 1)
    twice_in = right_of(jnp.where(lower, inverse, swapped), 0)
    lower = iota((examples * RANK, 2 * RANK), 1) < RANK
    held = grads[...]
    high = held.astype(BF16).astype(F32)
    thrice = jnp.concatenate([jnp.where(lower, high, held - high), high[:, :RANK]], axis=1)
    right_done = plain_dot(thrice.astype(BF16), twice_in, BY_COLUMNS)
    right_done = jnp.concatenate(
        [right_done[e * RANK : (e + 1) * RANK] for e in range(examples)], axis=1
    )
    lower = iota((RANK, 2 * RANK), 1) < RANK
    high = inverse.astype(BF16).astype(F32)
    swapped_high = pltpu.roll(high, RANK, 1)
    thrice = jnp.concatenate([jnp.where(lower, swapped_high, inverse - high), swapped_high[:, :RANK]], axis=1)
    done = plain_dot(thrice.astype(BF16), right_of(right_done, 0), BY_COLUMNS)
    for e in range(examples):
        turned[pl.ds(e * RANK, RANK), :] = done[:, e * 2 * RANK : (e + 1) * 2 * RANK]
    lower = iota((examples, 2 * RANK), 1) < RANK
    left = jnp.concatenate(
        [
            jnp.where(
                lower,
                turned[pl.ds(i, examples, stride=RANK), :],
                turned[pl.ds(i + 1, examples, stride=RANK), :],
            )
            for i in range(0, RANK, 2)
        ],
        axis=1,
    )
    high = left.astype(BF16).astype(F32)
    ahead[...] = jnp.concatenate([high, left - high], axis=0).astype(BF16)

    depth = 512

    def score(k, carry):
        main, rest = carry
        at = pl.ds(pl.multiple_of(k * depth, depth), depth)
        left = ahead[:, at]
        return (
            main + plain_dot(left, q_high[at, :], BY_COLUMNS),
            rest + plain_dot(left, q_low[at, :], BY_COLUMNS),
        )

    none = jnp.zeros((2 * examples, queries * DEVICES), F32)
    main, rest = lax.fori_loop(0, RANK * RANK // depth, score, (none, none))
    scores = main[:examples] + main[examples:] + rest[:examples]
    lane = iota((examples, DEVICES), 1)
    for h in range(queries):
        number = h * DEVICES // queries + lane // queries
        held_at = (number // SIDE) % 2 * (DEVICES // 2) + number // MEMBERS * SIDE + number % SIDE
        picked = [
            jnp.take_along_axis(scores[:, q * DEVICES : (q + 1) * DEVICES], held_at, axis=1)
            for q in range(queries)
        ]
        out[:, pl.ds(h * DEVICES, DEVICES)] = jnp.where(lane % queries == 0, picked[0], picked[1])

    for p in EVERYONE:
        wait_all(block(p, (others, 0, 0)), slab_send.at[p, 0])
        for d in STEPS:
            wait_all(block(p, (every, 0, 0)), slab_send.at[p, d])
            wait_all(block(p, (every, every, 0)), slab_send.at[p, 3 + d])
        wait_all(block(p, (every, every, every), 0), pair_send.at[p])
    wait_all(from_members, sum_send.at[0])
    wait_all(from_plane, sum_send.at[1])
    wait_all(from_members, sum_send.at[2])


def per_device(
    corpus_hidden,
    corpus_grad,
    corpus_lengths,
    query_hidden,
    query_grad,
    query_lengths,
    proj_in,
    proj_out,
):
    examples = corpus_hidden.shape[0]
    queries = query_hidden.shape[0]
    flat = lambda a: a.reshape(-1, a.shape[-1])
    anywhere = pl.BlockSpec(memory_space=pl.ANY)
    scalars = pl.BlockSpec(memory_space=pltpu.SMEM)
    operands = (
        flat(corpus_hidden),
        flat(corpus_grad),
        corpus_lengths,
        flat(query_hidden),
        flat(query_grad),
        query_lengths,
        proj_in.T,
        proj_out.T,
    )
    big = [operands[k] for k in (0, 1, 3, 4, 6, 7)]
    dma = pltpu.SemaphoreType.DMA
    steps = (proj_in.shape[0] + proj_out.shape[0]) // 1024
    scores = pl.pallas_call(
        kernel,
        out_shape=jax.ShapeDtypeStruct((examples, queries * DEVICES), F32),
        in_specs=[anywhere, anywhere, scalars, anywhere, anywhere, scalars, anywhere, anywhere],
        out_specs=pl.BlockSpec(memory_space=pltpu.VMEM),
        scratch_shapes=[pltpu.VMEM(a.shape, BF16) for a in big]
        + [
            pltpu.VMEM((examples * LEN, RANK), F32),
            pltpu.VMEM((examples * LEN, RANK), F32),
            pltpu.VMEM((queries * LEN, RANK), F32),
            pltpu.VMEM((queries * LEN, RANK), F32),
            pltpu.VMEM((examples * RANK, 2 * RANK), F32),
            pltpu.VMEM((2, SIDE, SIDE, SIDE, RANK, 2 * RANK), F32),
            pltpu.VMEM((RANK * RANK, queries * DEVICES), BF16),
            pltpu.VMEM((RANK * RANK, queries * DEVICES), BF16),
            pltpu.VMEM((RANK, 2 * RANK), F32),
            pltpu.VMEM((8, 2 * RANK), F32),
            pltpu.VMEM((MEMBERS - 1, 8, 2 * RANK), F32),
            pltpu.VMEM((CHIPS - 1, 8, 2 * RANK), F32),
            pltpu.VMEM((RANK, 2 * RANK), F32),
            pltpu.VMEM((examples * RANK, 2 * RANK), F32),
            pltpu.VMEM((2 * examples, RANK * RANK), BF16),
            dma((steps,)),
            dma((steps,)),
            dma((steps,)),
            dma((3,)),
            dma((3,)),
            dma((3, 7)),
            dma((3, 7)),
            dma((3,)),
            dma((3,)),
        ],
        compiler_params=pltpu.CompilerParams(
            collective_id=0, has_side_effects=True, vmem_limit_bytes=60 * 1024 * 1024
        ),
        name="influence",
    )(*operands)
    return scores


def solution(mesh):
    placed = (
        P(("corpus", "query"), None, None),
        P(("corpus", "query"), None, None),
        P(("corpus", "query")),
        P(("corpus", "query"), None, None),
        P(("corpus", "query"), None, None),
        P(("corpus", "query")),
        P(),
        P(),
    )
    return jax.shard_map(
        per_device,
        mesh=mesh,
        in_specs=placed,
        out_specs=P(("corpus", "query"), None),
        check_vma=False,
    )
```

time: 47.1 us -> 40.8 us (0.87)
  Pallas kernels: 45.4 us -> 39.3 us
    pallas_call x1, Pallas kernels: 45.4 us -> 39.3 us  [per_device(): pl.pallas_call(kernel, out_shape=jax.ShapeDtypeStruct((examples, queries...]
    reshape x2 -> x0, local copies, waits for them, and re-layouts: 1.51 us -> none  [per_device(): scores.reshape(examples, queries, DEVICES).transpose(0, 2, 1)]
    unnamed x0 -> x1, local copies, waits for them, and re-layouts: none -> 1.3 us
where the time goes in v2:
time: 40.8 us; the launch traced here: 40.6 us
  Pallas kernels  39.3 us (96%)
  local copies, waits for them, and re-layouts  1.3 us (3%)
    pallas_call x1, Pallas kernels, per_device(): pl.pallas_call(kernel, out_shape=jax.ShapeDtypeStruct((examples, queries...  39.3 us
    unnamed x1, local copies, waits for them, and re-layouts  1.3 us

profile of v2, /device:TPU:1, one launch (start us, length us, event | category | flops | bytes accessed | tf_op | source)
XLA Modules:
  0.0 40.6 jit_solution(212592191301048776)
XLA Ops:
  0.0 39.3 %influence.1 = f32[8,256]{1,0:T(8,128)} custom-call(bf16[512,14336]{1,0:T(8,128)(2,1)} %bitcast.6, bf16[512,4096]{1,0:T(8,128)(2,1)} %bitcast.7, s32[8]{0:T(128)} %corpus_lengths.1, bf16[128,14336]{1,0:T(8,128)(2,1)} %bitcast.8, bf16[128,4096]{1,0:T(8,128)(2,1)} %bitcast.10, s32[2]{0:T(128)} %query_lengths.1, bf16[64,14336]{1,0:T(8,128)(2,1)} %bitcast.9, ...), custom_call_target="tpu_custom_call" | custom-call | tf_op jit(solution)/shard_map/influence/pallas_call | solution.py:504
  39.3 1.3 %copy.10 = f32[8,256]{1,0:T(8,128)} copy(f32[8,256]{1,0:T(8,128)} %influence.1) | data formatting | bytes 16384

commit v3 on v2

--- a/solution.py
+++ b/solution.py
@@ -17,6 +17,7 @@
 CHIPS = SIDE * SIDE
 MEMBERS = 2 * SIDE
 DEVICES = CHIPS * MEMBERS
+SLAB = 72
 
 PARTS = ((0, 24, (2, 1, 0)), (24, 24, (1, 0, 2)), (48, 16, (0, 2, 1)))
 EVERYONE = range(len(PARTS))
@@ -381,25 +382,30 @@
 
     for d in STEPS[1:]:
         last_phase(d)
-    flat = slabs.reshape(DEVICES * RANK, 2 * RANK)
-
-    def halve(row):
-        q, i = row // half, row % half
-        high, low = split(flat[pl.ds(row, DEVICES, stride=RANK), :].T)
-        at = (
-            pl.ds(pl.multiple_of(i * 2 * RANK, 2 * RANK), 2 * RANK),
-            pl.ds(pl.multiple_of(q * DEVICES, DEVICES), DEVICES),
-        )
-        q_high[at] = high
-        q_low[at] = low
-
-    def halve_some(b):
-        for k in range(8):
-            halve(b * 8 + k)
-
+    flat = slabs.reshape(DEVICES * SLAB, 2 * RANK)
+
+    def halve(side, whose, i):
+        chips = DEVICES // 2
+        held = [
+            flat[pl.ds(whose * chips * SLAB + q * half + i, chips, stride=SLAB), :] for q in range(queries)
+        ]
+        high, low = split(jnp.concatenate(held, axis=0).T)
+        at = pl.ds(pl.multiple_of(i * 2 * RANK, 2 * RANK), 2 * RANK)
+        q_high[at, pl.ds(side * DEVICES, DEVICES)] = high
+        q_low[at, pl.ds(side * DEVICES, DEVICES)] = low
+
+    def halve_side(side, whose):
+        def some(b, carry):
+            for k in range(16):
+                halve(side, whose, b * 16 + k)
+            return carry
+
+        lax.fori_loop(0, half // 16, some, 0)
+
+    halve_side(0, core)
     for p in EVERYONE:
         wait_all(block(p, (every, every, every), 0), pair_recv.at[p])
-    lax.fori_loop(0, RANK // 8, lambda b, carry: (halve_some(b), carry)[1], 0)
+    halve_side(1, 1 - core)
 
     wait_all(from_members, sum_recv.at[2])
     pair = turned.at[pl.ds(0, RANK)]
@@ -422,14 +428,14 @@
     thrice = jnp.concatenate([jnp.where(lower, swapped_high, inverse - high), swapped_high[:, :RANK]], axis=1)
     done = plain_dot(thrice.astype(BF16), right_of(right_done, 0), BY_COLUMNS)
     for e in range(examples):
-        turned[pl.ds(e * RANK, RANK), :] = done[:, e * 2 * RANK : (e + 1) * 2 * RANK]
+        turned[pl.ds(e * SLAB, RANK), :] = done[:, e * 2 * RANK : (e + 1) * 2 * RANK]
     lower = iota((examples, 2 * RANK), 1) < RANK
     left = jnp.concatenate(
         [
             jnp.where(
                 lower,
-                turned[pl.ds(i, examples, stride=RANK), :],
-                turned[pl.ds(i + 1, examples, stride=RANK), :],
+                turned[pl.ds(i, examples, stride=SLAB), :],
+                turned[pl.ds(i + 1, examples, stride=SLAB), :],
             )
             for i in range(0, RANK, 2)
         ],
@@ -438,29 +444,20 @@
     high = left.astype(BF16).astype(F32)
     ahead[...] = jnp.concatenate([high, left - high], axis=0).astype(BF16)
 
-    depth = 512
-
-    def score(k, carry):
-        main, rest = carry
-        at = pl.ds(pl.multiple_of(k * depth, depth), depth)
-        left = ahead[:, at]
-        return (
-            main + plain_dot(left, q_high[at, :], BY_COLUMNS),
-            rest + plain_dot(left, q_low[at, :], BY_COLUMNS),
-        )
-
-    none = jnp.zeros((2 * examples, queries * DEVICES), F32)
-    main, rest = lax.fori_loop(0, RANK * RANK // depth, score, (none, none))
+    left = ahead[...]
+    main = plain_dot(left, q_high[...], BY_COLUMNS)
+    rest = plain_dot(left, q_low[...], BY_COLUMNS)
     scores = main[:examples] + main[examples:] + rest[:examples]
     lane = iota((examples, DEVICES), 1)
+    ours = lane // MEMBERS % 2 == core
     for h in range(queries):
-        number = h * DEVICES // queries + lane // queries
-        held_at = (number // SIDE) % 2 * (DEVICES // 2) + number // MEMBERS * SIDE + number % SIDE
+        place_of = h * MEMBERS + lane // (2 * MEMBERS)
+        held_at = lane % queries * (DEVICES // 2) + place_of * SIDE + lane // queries % SIDE
         picked = [
-            jnp.take_along_axis(scores[:, q * DEVICES : (q + 1) * DEVICES], held_at, axis=1)
-            for q in range(queries)
+            jnp.take_along_axis(scores[:, k * DEVICES : (k + 1) * DEVICES], held_at, axis=1)
+            for k in range(2)
         ]
-        out[:, pl.ds(h * DEVICES, DEVICES)] = jnp.where(lane % queries == 0, picked[0], picked[1])
+        out[:, pl.ds(h * DEVICES, DEVICES)] = jnp.where(ours, picked[0], picked[1])
 
     for p in EVERYONE:
         wait_all(block(p, (others, 0, 0)), slab_send.at[p, 0])
@@ -513,7 +510,7 @@
             pltpu.VMEM((queries * LEN, RANK), F32),
             pltpu.VMEM((queries * LEN, RANK), F32),
             pltpu.VMEM((examples * RANK, 2 * RANK), F32),
-            pltpu.VMEM((2, SIDE, SIDE, SIDE, RANK, 2 * RANK), F32),
+            pltpu.VMEM((2, SIDE, SIDE, SIDE, SLAB, 2 * RANK), F32),
             pltpu.VMEM((RANK * RANK, queries * DEVICES), BF16),
             pltpu.VMEM((RANK * RANK, queries * DEVICES), BF16),
             pltpu.VMEM((RANK, 2 * RANK), F32),
@@ -521,7 +518,7 @@
             pltpu.VMEM((MEMBERS - 1, 8, 2 * RANK), F32),
             pltpu.VMEM((CHIPS - 1, 8, 2 * RANK), F32),
             pltpu.VMEM((RANK, 2 * RANK), F32),
-            pltpu.VMEM((examples * RANK, 2 * RANK), F32),
+            pltpu.VMEM((examples * SLAB, 2 * RANK), F32),
             pltpu.VMEM((2 * examples, RANK * RANK), BF16),
             dma((steps,)),
             dma((steps,)),

time: 40.8 us -> 37.4 us (0.917)
  Pallas kernels: 39.3 us -> 35.9 us
    pallas_call x1, Pallas kernels: 39.3 us -> 35.9 us  [per_device(): pl.pallas_call(kernel, out_shape=jax.ShapeDtypeStruct((examples, queries...]
where the time goes in v3:
time: 37.4 us; the launch traced here: 37.2 us
  Pallas kernels  35.9 us (96%)
  local copies, waits for them, and re-layouts  1.3 us (3%)
    pallas_call x1, Pallas kernels, per_device(): pl.pallas_call(kernel, out_shape=jax.ShapeDtypeStruct((examples, queries...  35.9 us
    unnamed x1, local copies, waits for them, and re-layouts  1.3 us

profile of v3, /device:TPU:1, one launch (start us, length us, event | category | flops | bytes accessed | tf_op | source)
XLA Modules:
  0.0 37.2 jit_solution(9556950946974960529)
XLA Ops:
  0.0 35.9 %influence.1 = f32[8,256]{1,0:T(8,128)} custom-call(bf16[512,14336]{1,0:T(8,128)(2,1)} %bitcast.6, bf16[512,4096]{1,0:T(8,128)(2,1)} %bitcast.7, s32[8]{0:T(128)} %corpus_lengths.1, bf16[128,14336]{1,0:T(8,128)(2,1)} %bitcast.8, bf16[128,4096]{1,0:T(8,128)(2,1)} %bitcast.10, s32[2]{0:T(128)} %query_lengths.1, bf16[64,14336]{1,0:T(8,128)(2,1)} %bitcast.9, ...), custom_call_target="tpu_custom_call" | custom-call | tf_op jit(solution)/shard_map/influence/pallas_call | solution.py:501
  35.9 1.3 %copy.10 = f32[8,256]{1,0:T(8,128)} copy(f32[8,256]{1,0:T(8,128)} %influence.1) | data formatting | bytes 16384

commit v4 on v3

--- a/solution.py
+++ b/solution.py
@@ -360,7 +360,7 @@
 
     for d in range(1, MEMBERS):
         send_sum(0, part.at[octet((member + d) % MEMBERS)], from_members.at[d - 1], member_at(d))
-    for d in STEPS:
+    for d in STEPS[:2]:
         third_phase(d)
     for e in range(0, examples, 2):
         tokens = slice(e * LEN, (e + 2) * LEN)
@@ -372,7 +372,7 @@
     piece[...] = total
     for d in range(1, CHIPS):
         send_sum(1, piece, from_plane.at[d - 1], place_at(d))
-    last_phase(1)
+    third_phase(STEPS[2])
     wait_all(from_plane, sum_recv.at[1])
     for d in range(CHIPS - 1):
         total = total + from_plane[d]
@@ -380,7 +380,7 @@
     for d in range(1, MEMBERS):
         send_sum(2, fisher.at[octet(member)], fisher.at[octet(member)], member_at(d))
 
-    for d in STEPS[1:]:
+    for d in STEPS:
         last_phase(d)
     flat = slabs.reshape(DEVICES * SLAB, 2 * RANK)
 
@@ -403,14 +403,14 @@
         lax.fori_loop(0, half // 16, some, 0)
 
     halve_side(0, core)
-    for p in EVERYONE:
-        wait_all(block(p, (every, every, every), 0), pair_recv.at[p])
-    halve_side(1, 1 - core)
 
     wait_all(from_members, sum_recv.at[2])
     pair = turned.at[pl.ds(0, RANK)]
     pair[...] = damp(fisher[...])
     invert_pair(pair)
+    for p in EVERYONE:
+        wait_all(block(p, (every, every, every), 0), pair_recv.at[p])
+    halve_side(1, 1 - core)
     inverse = pair[...]
     swapped = pltpu.roll(inverse, RANK, 1)
     twice_in = right_of(jnp.where(lower, inverse, swapped), 0)
@@ -500,7 +500,7 @@
     steps = (proj_in.shape[0] + proj_out.shape[0]) // 1024
     scores = pl.pallas_call(
         kernel,
-        out_shape=jax.ShapeDtypeStruct((examples, queries * DEVICES), F32),
+        out_shape=pltpu.VMEM((examples, queries * DEVICES), F32),
         in_specs=[anywhere, anywhere, scalars, anywhere, anywhere, scalars, anywhere, anywhere],
         out_specs=pl.BlockSpec(memory_space=pltpu.VMEM),
         scratch_shapes=[pltpu.VMEM(a.shape, BF16) for a in big]

time: 37.4 us -> 35.4 us (0.947)
  Pallas kernels: 35.9 us -> 34.6 us
  local copies, waits for them, and re-layouts: 1.3 us -> 0.6 us
    pallas_call x1, Pallas kernels: 35.9 us -> 34.6 us  [per_device(): pl.pallas_call(kernel, out_shape=pltpu.VMEM((examples, queries * DEVICES)...]
    unnamed x1, local copies, waits for them, and re-layouts: 1.3 us -> 0.6 us
where the time goes in v4:
time: 35.4 us; the launch traced here: 35.2 us
  Pallas kernels  34.6 us (98%)
  local copies, waits for them, and re-layouts  0.6 us (2%)
    pallas_call x1, Pallas kernels, per_device(): pl.pallas_call(kernel, out_shape=pltpu.VMEM((examples, queries * DEVICES)...  34.6 us

profile of v4, /device:TPU:1, one launch (start us, length us, event | category | flops | bytes accessed | tf_op | source)
XLA Modules:
  0.0 35.2 jit_solution(656863564970594876)
XLA Ops:
  0.0 34.6 %influence.1 = f32[8,256]{1,0:T(8,128)S(1)} custom-call(bf16[512,14336]{1,0:T(8,128)(2,1)} %bitcast.6, bf16[512,4096]{1,0:T(8,128)(2,1)} %bitcast.7, s32[8]{0:T(128)} %corpus_lengths.1, bf16[128,14336]{1,0:T(8,128)(2,1)} %bitcast.8, bf16[128,4096]{1,0:T(8,128)(2,1)} %bitcast.10, s32[2]{0:T(128)} %query_lengths.1, bf16[64,14336]{1,0:T(8,128)(2,1)} %bitcast.9, ...), custom_call_target="tpu_custom_call" | custom-call | tf_op jit(solution)/shard_map/influence/pallas_call | solution.py:501
  34.6 0.6 %copy.10 = f32[8,256]{1,0:T(8,128)} copy(f32[8,256]{1,0:T(8,128)S(1)} %influence.1) | data formatting | bytes 16384

commit v5 on v4

--- a/solution.py
+++ b/solution.py
@@ -360,8 +360,7 @@
 
     for d in range(1, MEMBERS):
         send_sum(0, part.at[octet((member + d) % MEMBERS)], from_members.at[d - 1], member_at(d))
-    for d in STEPS[:2]:
-        third_phase(d)
+    third_phase(STEPS[0])
     for e in range(0, examples, 2):
         tokens = slice(e * LEN, (e + 2) * LEN)
         grads[pl.ds(e * RANK, 2 * RANK), :] = gradients(both[RANK:, tokens], both[:RANK, tokens])
@@ -372,7 +371,8 @@
     piece[...] = total
     for d in range(1, CHIPS):
         send_sum(1, piece, from_plane.at[d - 1], place_at(d))
-    third_phase(STEPS[2])
+    for d in STEPS[1:]:
+        third_phase(d)
     wait_all(from_plane, sum_recv.at[1])
     for d in range(CHIPS - 1):
         total = total + from_plane[d]
@@ -382,7 +382,7 @@
 
     for d in STEPS:
         last_phase(d)
-    flat = slabs.reshape(DEVICES * SLAB, 2 * RANK)
+    flat = slabs.reshape(3 * DEVICES // 2 * SLAB, 2 * RANK)
 
     def halve(side, whose, i):
         chips = DEVICES // 2
@@ -510,7 +510,7 @@
             pltpu.VMEM((queries * LEN, RANK), F32),
             pltpu.VMEM((queries * LEN, RANK), F32),
             pltpu.VMEM((examples * RANK, 2 * RANK), F32),
-            pltpu.VMEM((2, SIDE, SIDE, SIDE, SLAB, 2 * RANK), F32),
+            pltpu.VMEM((3, SIDE, SIDE, SIDE, SLAB, 2 * RANK), F32),
             pltpu.VMEM((RANK * RANK, queries * DEVICES), BF16),
             pltpu.VMEM((RANK * RANK, queries * DEVICES), BF16),
             pltpu.VMEM((RANK, 2 * RANK), F32),
@@ -518,7 +518,7 @@
             pltpu.VMEM((MEMBERS - 1, 8, 2 * RANK), F32),
             pltpu.VMEM((CHIPS - 1, 8, 2 * RANK), F32),
             pltpu.VMEM((RANK, 2 * RANK), F32),
-            pltpu.VMEM((examples * SLAB, 2 * RANK), F32),
+            pltpu.VMEM(((examples + 1) * SLAB, 2 * RANK), F32),
             pltpu.VMEM((2 * examples, RANK * RANK), BF16),
             dma((steps,)),
             dma((steps,)),

time: 35.4 us -> 35.2 us (level)
  no operation moved by 1% of the time
where the time goes in v5:
time: 35.2 us; the launch traced here: 35.1 us
  Pallas kernels  34.5 us (98%)
  local copies, waits for them, and re-layouts  0.6 us (2%)
    pallas_call x1, Pallas kernels, per_device(): pl.pallas_call(kernel, out_shape=pltpu.VMEM((examples, queries * DEVICES)...  34.5 us

profile of v5, /device:TPU:1, one launch (start us, length us, event | category | flops | bytes accessed | tf_op | source)
XLA Modules:
  0.0 35.1 jit_solution(14693672017406742881)
XLA Ops:
  0.0 34.5 %influence.1 = f32[8,256]{1,0:T(8,128)S(1)} custom-call(bf16[512,14336]{1,0:T(8,128)(2,1)} %bitcast.6, bf16[512,4096]{1,0:T(8,128)(2,1)} %bitcast.7, s32[8]{0:T(128)} %corpus_lengths.1, bf16[128,14336]{1,0:T(8,128)(2,1)} %bitcast.8, bf16[128,4096]{1,0:T(8,128)(2,1)} %bitcast.10, s32[2]{0:T(128)} %query_lengths.1, bf16[64,14336]{1,0:T(8,128)(2,1)} %bitcast.9, ...), custom_call_target="tpu_custom_call" | custom-call | tf_op jit(solution)/shard_map/influence/pallas_call | solution.py:501
  34.5 0.6 %copy.10 = f32[8,256]{1,0:T(8,128)} copy(f32[8,256]{1,0:T(8,128)S(1)} %influence.1) | data formatting | bytes 16384
